TPU v7x, 128 devices: a whole 4x4x4 slice. The times are simulated.
128 devices in a mesh: role: 2 (over core), dp: 64 (over y, z, x).
Axes of the slice: x: 4, y: 4, z: 4, core: 2. Of those that a mesh axis runs over, the one named last changes fastest.
Arguments:
- patch_rows: bfloat16 [81920, 768], P(('role', 'dp')), may hold values from -6 to 6
- patch_order: int32 [1024, 196], replicated, may hold values from 0 to 195, each once within a row
- visible_count: int32 [1024], replicated, may hold values from 20 to 78, as said below
- encoded_image: int32 [1024], replicated, may hold values from 0 to 1023, as said below
- first_gain: bfloat16 [768], P(('role', 'dp')), may hold values from 0.5 to 1.5
- first_shift: bfloat16 [768], P(('role', 'dp')), may hold values from -1.75 to 1.75
- query_key_value: bfloat16 [768, 2304], P(('role', 'dp')), may hold values from -0.21875 to 0.21875
- query_bias: bfloat16 [768], P(('role', 'dp')), may hold values from -1.75 to 1.75
- value_bias: bfloat16 [768], P(('role', 'dp')), may hold values from -1.75 to 1.75
- output_weight: bfloat16 [768, 768], P(('role', 'dp')), may hold values from -1.5 to 1.5
- output_bias: bfloat16 [768], P(('role', 'dp')), may hold values from -1.75 to 1.75
- second_gain: bfloat16 [768], P(('role', 'dp')), may hold values from 0.5 to 1.5
- second_shift: bfloat16 [768], P(('role', 'dp')), may hold values from -1.75 to 1.75
- up_weight: bfloat16 [768, 3072], P(('role', 'dp')), may hold values from -0.21875 to 0.21875
- up_bias: bfloat16 [3072], P(('role', 'dp')), may hold values from -1.75 to 1.75
- down_weight: bfloat16 [3072, 768], P(('role', 'dp')), may hold values from -0.109375 to 0.109375
- down_bias: bfloat16 [768], P(('role', 'dp')), may hold values from -1.75 to 1.75
- embed_weight: bfloat16 [768, 512], P(('role', 'dp')), may hold values from -0.21875 to 0.21875
- embed_bias: bfloat16 [512], P(('role', 'dp')), may hold values from -1.75 to 1.75
- mask_token: bfloat16 [512], P(('role', 'dp')), may hold values from -6 to 6
- decoder_gain: bfloat16 [512], P(('role', 'dp')), may hold values from 0.5 to 1.5
- decoder_shift: bfloat16 [512], P(('role', 'dp')), may hold values from -1.75 to 1.75
- pixel_weight: bfloat16 [512, 768], P(('role', 'dp')), may hold values from -0.25 to 0.25
- pixel_bias: bfloat16 [768], P(('role', 'dp')), may hold values from -1.75 to 1.75
- pixel_grad: bfloat16 [1024, 196, 768], P(('role', 'dp')), may hold values from -6 to 6
Outputs:
- pixels: bfloat16 [1024, 196, 768], P(('role', 'dp'))
- patch_grad: bfloat16 [81920, 768], P(('role', 'dp'))
- first_gain_grad: float32 [768], P(('role', 'dp'))
- first_shift_grad: float32 [768], P(('role', 'dp'))
- query_key_value_grad: float32 [768, 2304], P(('role', 'dp'))
- query_bias_grad: float32 [768], P(('role', 'dp'))
- value_bias_grad: float32 [768], P(('role', 'dp'))
- output_weight_grad: float32 [768, 768], P(('role', 'dp'))
- output_bias_grad: float32 [768], P(('role', 'dp'))
- second_gain_grad: float32 [768], P(('role', 'dp'))
- second_shift_grad: float32 [768], P(('role', 'dp'))
- up_weight_grad: float32 [768, 3072], P(('role', 'dp'))
- up_bias_grad: float32 [3072], P(('role', 'dp'))
- down_weight_grad: float32 [3072, 768], P(('role', 'dp'))
- down_bias_grad: float32 [768], P(('role', 'dp'))
- embed_weight_grad: float32 [768, 512], P(('role', 'dp'))
- embed_bias_grad: float32 [512], P(('role', 'dp'))
- mask_token_grad: float32 [512], P(('role', 'dp'))
- decoder_gain_grad: float32 [512], P(('role', 'dp'))
- decoder_shift_grad: float32 [512], P(('role', 'dp'))
- pixel_weight_grad: float32 [512, 768], P(('role', 'dp'))
- pixel_bias_grad: float32 [768], P(('role', 'dp'))
Inputs may be any that keep to these rules, and one draw needn't show every extreme that they name: `visible_count`: some image has exactly 20 visible patches and some exactly 78. `encoded_image`: each image stands once; slot j is on device j // 8 (devices counted over role and dp, role first); with that device at role index r and dp index p, the image of slot j has its grid on the device at role index 1 - r and dp index (p + j % 8) % 64, and the grid of image i is on device i // 8.
All inputs are finite; a program needn't handle non-finite values.
Results may differ from a plain program's by a relative error of at most 0.019.
Values may be sent and summed in bfloat16 or wider, within the bound.
No kernel may reach another device: no remote copies, remote signals or barrier semaphores. Data moves between devices by JAX's collectives and lax.ppermute only.
A program may use at most 256 MiB of HBM per device.

v0:
```python
import jax
import jax.numpy as jnp
from jax import lax
from jax.sharding import PartitionSpec as P

D = 768
H = 12
HD = 64
DD = 512
PIX = 768
SIDE = 14
SLOT = 80
IMG_DEV = 8
GRID = 196


epsilon = 1e-06
masked_score = -1e30


def passed_along(array, axis, by):
    count = lax.axis_size(axis)
    return lax.ppermute(array, axis, [(i, (i + by) % count) for i in range(count)])


def joined_along(pieces, dim):
    shape = list(pieces.shape[1:])
    shape[dim] *= pieces.shape[0]
    return jnp.moveaxis(pieces, 0, dim).reshape(shape)


def gather_together(arrays, axis, dims):
    line = jnp.concatenate([a.reshape(-1) for a in arrays])
    lines, at, gathered = (lax.all_gather(line, axis), 0, [])
    for a, dim in zip(arrays, dims):
        pieces = lines[:, at : at + a.size].reshape(-1, *a.shape)
        gathered.append(joined_along(pieces, dim))
        at += a.size
    return tuple(gathered)


def swapped(array, axis, apart):
    return lax.ppermute(array, axis, [(i, i ^ 1 << apart) for i in range(lax.axis_size(axis))])


def layer_norm(values, gain, shift):
    average = jnp.mean(values, axis=-1, keepdims=True)
    centered = values - average
    variance = jnp.mean(centered * centered, axis=-1, keepdims=True)
    return centered * lax.rsqrt(variance + epsilon) * gain + shift


def positions():
    quarter = DD // 4
    frequency = 10000.0 ** (-jnp.arange(quarter, dtype=jnp.float32) / quarter)
    places = jnp.arange(GRID, dtype=jnp.int32)
    row_angle = (places // SIDE).astype(jnp.float32)[:, None] * frequency[None, :]
    col_angle = (places % SIDE).astype(jnp.float32)[:, None] * frequency[None, :]
    return jnp.concatenate(
        [jnp.sin(row_angle), jnp.cos(row_angle), jnp.sin(col_angle), jnp.cos(col_angle)], axis=1
    )


def smooth_gate(values):
    return jax.nn.gelu(values, approximate=True)


def transpose_dot(left, right):
    return lax.dot_general(
        left, right, (((0,), (0,)), ((), ())), preferred_element_type=jnp.float32
    )


def dot_right(left, right):
    return lax.dot_general(
        left, right, (((1,), (1,)), ((), ())), preferred_element_type=jnp.float32
    )


def plain_dot(left, right):
    return jnp.dot(left, right, preferred_element_type=jnp.float32)


def column_sum(values):
    return jnp.sum(values.astype(jnp.float32), axis=0)


def move_out(piece, step):
    return passed_along(piece, "dp", step)


def move_back(piece, step):
    return passed_along(piece, "dp", -step)


def body(
    patch_rows,
    patch_order,
    visible_count,
    encoded_image,
    first_gain,
    first_shift,
    query_key_value,
    query_bias,
    value_bias,
    output_weight,
    output_bias,
    second_gain,
    second_shift,
    up_weight,
    up_bias,
    down_weight,
    down_bias,
    embed_weight,
    embed_bias,
    mask_token,
    decoder_gain,
    decoder_shift,
    pixel_weight,
    pixel_bias,
    pixel_grad,
):
    gathered = gather_together(
        (
            first_gain,
            first_shift,
            query_key_value,
            query_bias,
            value_bias,
            output_weight,
            output_bias,
            second_gain,
            second_shift,
            up_weight,
            up_bias,
            down_weight,
            down_bias,
            embed_weight,
            embed_bias,
            mask_token,
            decoder_gain,
            decoder_shift,
            pixel_weight,
            pixel_bias,
        ),
        ("role", "dp"),
        (0, 0, 0, 0, 0, 0, 0, 0, 0, 0, 0, 0, 0, 0, 0, 0, 0, 0, 0, 0),
    )
    (
        gain_one,
        shift_one,
        mix_weight,
        bias_query,
        bias_value,
        out_weight,
        out_bias,
        gain_two,
        shift_two,
        hidden_weight,
        hidden_bias,
        back_weight,
        back_bias,
        emb_weight,
        emb_bias,
        token_mask,
        gain_three,
        shift_three,
        pix_weight,
        pix_bias,
    ) = gathered
    gain_one = gain_one.astype(jnp.float32)
    shift_one = shift_one.astype(jnp.float32)
    gain_two = gain_two.astype(jnp.float32)
    shift_two = shift_two.astype(jnp.float32)
    gain_three = gain_three.astype(jnp.float32)
    shift_three = shift_three.astype(jnp.float32)
    device = lax.axis_index(("role", "dp"))
    row_count = IMG_DEV * SLOT
    image_count = encoded_image.shape[0]
    scale = HD ** (-0.5)
    held = lax.dynamic_slice_in_dim(encoded_image, device * IMG_DEV, IMG_DEV)
    matches = held[:, None] == jnp.arange(image_count, dtype=jnp.int32)[None, :]
    held_count = jnp.sum(jnp.where(matches, visible_count[None, :], 0), axis=1)
    live_slot = jnp.arange(SLOT, dtype=jnp.int32)[None, :] < held_count[:, None]
    shape_four = (IMG_DEV, SLOT, H, HD)
    inputs = patch_rows.astype(jnp.float32)
    normed_low = layer_norm(inputs, gain_one, shift_one).astype(jnp.bfloat16)
    bias_mix = jnp.concatenate(
        [
            bias_query.astype(jnp.float32),
            jnp.zeros((D,), jnp.float32),
            bias_value.astype(jnp.float32),
        ]
    )
    mixed = (plain_dot(normed_low, mix_weight) + bias_mix).astype(jnp.bfloat16)
    queries = mixed[:, :D].reshape(shape_four)
    keys_all = mixed[:, D : 2 * D].reshape(shape_four)
    values_all = mixed[:, 2 * D :].reshape(shape_four)

    def scores_of():
        raw_scores = (
            jnp.einsum("sqhe,skhe->shqk", queries, keys_all, preferred_element_type=jnp.float32)
            * scale
        )
        return jnp.where(live_slot[:, None, None, :], raw_scores, masked_score)

    scores = scores_of()
    top_score = jnp.max(scores, axis=-1, keepdims=True)
    shifted = jnp.exp(scores - top_score)
    total = jnp.sum(shifted, axis=-1, keepdims=True)
    log_total = top_score + jnp.log(total)
    probs_low = (shifted / total).astype(jnp.bfloat16)
    attended = (
        jnp.einsum("shqk,skhe->sqhe", probs_low, values_all, preferred_element_type=jnp.float32)
        .reshape(row_count, D)
        .astype(jnp.bfloat16)
    )
    resid = inputs + (plain_dot(attended, out_weight) + out_bias.astype(jnp.float32))
    normed_two_low = layer_norm(resid, gain_two, shift_two).astype(jnp.bfloat16)
    hidden = plain_dot(normed_two_low, hidden_weight) + hidden_bias.astype(jnp.float32)
    active_low = smooth_gate(hidden).astype(jnp.bfloat16)
    encoded = resid + (plain_dot(active_low, back_weight) + back_bias.astype(jnp.float32))
    encoded_low = encoded.astype(jnp.bfloat16)
    embedded = (plain_dot(encoded_low, emb_weight) + emb_bias.astype(jnp.float32)).astype(
        jnp.bfloat16
    )
    blocks = embedded.reshape(IMG_DEV, SLOT, DD)
    own_images = device * IMG_DEV + jnp.arange(IMG_DEV, dtype=jnp.int32)
    found = encoded_image[None, :] == own_images[:, None]
    source_slot = jnp.sum(
        jnp.where(found, jnp.arange(image_count, dtype=jnp.int32)[None, :], 0), axis=1
    )
    source_place = source_slot % IMG_DEV
    crossed = swapped(blocks, "role", 0)
    received = jnp.stack(
        [crossed[0]] + [move_out(crossed[step], step) for step in range(1, IMG_DEV)]
    )
    arrived = received[source_place]
    own_count = lax.dynamic_slice_in_dim(visible_count, device * IMG_DEV, IMG_DEV)
    own_order = lax.dynamic_slice_in_dim(patch_order, device * IMG_DEV, IMG_DEV, 0)[:, :SLOT]
    placement = (own_order[:, None, :] == jnp.arange(GRID, dtype=jnp.int32)[None, :, None]) & (
        jnp.arange(SLOT, dtype=jnp.int32)[None, None, :] < own_count[:, None, None]
    )
    place_low = placement.astype(jnp.bfloat16)
    masked_share = 1.0 - jnp.sum(placement.astype(jnp.float32), axis=2)
    grid = (
        jnp.einsum("pgt,ptc->pgc", place_low, arrived, preferred_element_type=jnp.float32)
        + masked_share[..., None] * token_mask.astype(jnp.float32)
        + positions()[None]
    )
    decoded_low = (
        layer_norm(grid, gain_three, shift_three).astype(jnp.bfloat16).reshape(IMG_DEV * GRID, DD)
    )
    pixels = (
        (plain_dot(decoded_low, pix_weight) + pix_bias.astype(jnp.float32))
        .astype(jnp.bfloat16)
        .reshape(IMG_DEV, GRID, PIX)
    )
    upstream = pixel_grad.reshape(IMG_DEV * GRID, PIX)
    grad_pixel_weight = transpose_dot(decoded_low, upstream)
    grad_pixel_bias = column_sum(upstream)
    grad_decoded = dot_right(upstream, pix_weight).reshape(IMG_DEV, GRID, DD)
    grid_back = jax.vjp(layer_norm, grid, gain_three, shift_three)[1]
    grad_grid, grad_decoder_gain, grad_decoder_shift = grid_back(grad_decoded)
    grad_mask_token = jnp.sum(masked_share[..., None] * grad_grid, axis=(0, 1))
    grad_rows = jnp.einsum(
        "pgt,pgc->ptc",
        place_low,
        grad_grid.astype(jnp.bfloat16),
        preferred_element_type=jnp.float32,
    ).astype(jnp.bfloat16)
    placed = jnp.zeros((IMG_DEV, SLOT, DD), jnp.bfloat16).at[source_place].set(grad_rows)
    stepped = jnp.stack([placed[0]] + [move_back(placed[step], step) for step in range(1, IMG_DEV)])
    came_home = swapped(stepped, "role", 0)
    grad_embedded = came_home.reshape(row_count, DD)
    grad_embed_weight = transpose_dot(encoded_low, grad_embedded)
    grad_embed_bias = column_sum(grad_embedded)
    grad_encoded = dot_right(grad_embedded, emb_weight)
    grad_branch_two = grad_encoded.astype(jnp.bfloat16)
    grad_down_weight = transpose_dot(active_low, grad_branch_two)
    grad_down_bias = column_sum(grad_branch_two)
    grad_active = dot_right(grad_branch_two, back_weight)
    gate_back = jax.vjp(smooth_gate, hidden)[1]
    grad_hidden = gate_back(grad_active)[0].astype(jnp.bfloat16)
    grad_up_weight = transpose_dot(normed_two_low, grad_hidden)
    grad_up_bias = column_sum(grad_hidden)
    grad_normed_two = dot_right(grad_hidden, hidden_weight)
    resid_back = jax.vjp(layer_norm, resid, gain_two, shift_two)[1]
    grad_resid_part, grad_second_gain, grad_second_shift = resid_back(grad_normed_two)
    grad_resid = grad_encoded + grad_resid_part
    grad_branch = grad_resid.astype(jnp.bfloat16)
    grad_output_weight = transpose_dot(attended, grad_branch)
    grad_output_bias = column_sum(grad_branch)
    grad_attended = dot_right(grad_branch, out_weight).astype(jnp.bfloat16).reshape(shape_four)
    probs_again = jnp.exp(scores_of() - log_total)
    grad_probs = jnp.einsum(
        "sqhe,skhe->shqk", grad_attended, values_all, preferred_element_type=jnp.float32
    )
    grad_values = jnp.einsum(
        "shqk,sqhe->skhe",
        probs_again.astype(jnp.bfloat16),
        grad_attended,
        preferred_element_type=jnp.float32,
    )
    grad_scores = (
        probs_again * (grad_probs - jnp.sum(probs_again * grad_probs, axis=-1, keepdims=True))
    ).astype(jnp.bfloat16)
    grad_queries = (
        jnp.einsum("shqk,skhe->sqhe", grad_scores, keys_all, preferred_element_type=jnp.float32)
        * scale
    )
    grad_keys = (
        jnp.einsum("shqk,sqhe->skhe", grad_scores, queries, preferred_element_type=jnp.float32)
        * scale
    )
    grad_mixed = jnp.concatenate(
        [
            grad_queries.reshape(row_count, D),
            grad_keys.reshape(row_count, D),
            grad_values.reshape(row_count, D),
        ],
        axis=1,
    ).astype(jnp.bfloat16)
    grad_mix_weight = transpose_dot(normed_low, grad_mixed)
    grad_query_bias = column_sum(grad_mixed[:, :D])
    grad_value_bias = column_sum(grad_mixed[:, 2 * D :])
    grad_normed = dot_right(grad_mixed, mix_weight)
    input_back = jax.vjp(layer_norm, inputs, gain_one, shift_one)[1]
    grad_input_part, grad_first_gain, grad_first_shift = input_back(grad_normed)
    patch_grad = (grad_resid + grad_input_part).astype(jnp.bfloat16)
    shards = tuple(
        (
            lax.psum_scatter(grad_first_gain, ("role", "dp"), scatter_dimension=0, tiled=True),
            lax.psum_scatter(grad_first_shift, ("role", "dp"), scatter_dimension=0, tiled=True),
            lax.psum_scatter(grad_mix_weight, ("role", "dp"), scatter_dimension=0, tiled=True),
            lax.psum_scatter(grad_query_bias, ("role", "dp"), scatter_dimension=0, tiled=True),
            lax.psum_scatter(grad_value_bias, ("role", "dp"), scatter_dimension=0, tiled=True),
            lax.psum_scatter(grad_output_weight, ("role", "dp"), scatter_dimension=0, tiled=True),
            lax.psum_scatter(grad_output_bias, ("role", "dp"), scatter_dimension=0, tiled=True),
            lax.psum_scatter(grad_second_gain, ("role", "dp"), scatter_dimension=0, tiled=True),
            lax.psum_scatter(grad_second_shift, ("role", "dp"), scatter_dimension=0, tiled=True),
            lax.psum_scatter(grad_up_weight, ("role", "dp"), scatter_dimension=0, tiled=True),
            lax.psum_scatter(grad_up_bias, ("role", "dp"), scatter_dimension=0, tiled=True),
            lax.psum_scatter(grad_down_weight, ("role", "dp"), scatter_dimension=0, tiled=True),
            lax.psum_scatter(grad_down_bias, ("role", "dp"), scatter_dimension=0, tiled=True),
            lax.psum_scatter(grad_embed_weight, ("role", "dp"), scatter_dimension=0, tiled=True),
            lax.psum_scatter(grad_embed_bias, ("role", "dp"), scatter_dimension=0, tiled=True),
            lax.psum_scatter(grad_mask_token, ("role", "dp"), scatter_dimension=0, tiled=True),
            lax.psum_scatter(grad_decoder_gain, ("role", "dp"), scatter_dimension=0, tiled=True),
            lax.psum_scatter(grad_decoder_shift, ("role", "dp"), scatter_dimension=0, tiled=True),
            lax.psum_scatter(grad_pixel_weight, ("role", "dp"), scatter_dimension=0, tiled=True),
            lax.psum_scatter(grad_pixel_bias, ("role", "dp"), scatter_dimension=0, tiled=True),
        )
    )
    return (pixels, patch_grad) + shards


def solution(mesh):
    placed = (
        P(("role", "dp"), None),
        P(),
        P(),
        P(),
        P(("role", "dp")),
        P(("role", "dp")),
        P(("role", "dp"), None),
        P(("role", "dp")),
        P(("role", "dp")),
        P(("role", "dp"), None),
        P(("role", "dp")),
        P(("role", "dp")),
        P(("role", "dp")),
        P(("role", "dp"), None),
        P(("role", "dp")),
        P(("role", "dp"), None),
        P(("role", "dp")),
        P(("role", "dp"), None),
        P(("role", "dp")),
        P(("role", "dp")),
        P(("role", "dp")),
        P(("role", "dp")),
        P(("role", "dp"), None),
        P(("role", "dp")),
        P(("role", "dp"), None, None),
    )
    return jax.shard_map(
        body,
        mesh=mesh,
        in_specs=placed,
        out_specs=(
            P(("role", "dp"), None, None),
            P(("role", "dp"), None),
            P(("role", "dp")),
            P(("role", "dp")),
            P(("role", "dp"), None),
            P(("role", "dp")),
            P(("role", "dp")),
            P(("role", "dp"), None),
            P(("role", "dp")),
            P(("role", "dp")),
            P(("role", "dp")),
            P(("role", "dp"), None),
            P(("role", "dp")),
            P(("role", "dp"), None),
            P(("role", "dp")),
            P(("role", "dp"), None),
            P(("role", "dp")),
            P(("role", "dp")),
            P(("role", "dp")),
            P(("role", "dp")),
            P(("role", "dp"), None),
            P(("role", "dp")),
        ),
        check_vma=False,
    )
```

profile of v0, /device:TPU:8, one launch (start us, length us, event | category | flops | bytes accessed | tf_op | source)
XLA Modules:
  0.0 1659.5 jit_solution(3072637041134665278)
XLA Ops:
  12.0 11.9 concatenate.13
  42.7 208.0 %all-reduce.29.cloned.1.call-done = bf16[7876352]{0:T(1024)(128)(2,1)} async-done(((bf16[7876352]{0:T(1024)(128)(2,1)}), bf16[7876352]{0:T(1024)(128)(2,1)}) %all-reduce.29.cloned.1.call-update) | async-done | bytes 15752720
  250.7 37.9 %reshape.483 = bf16[128,61534]{1,0:T(8,128)(2,1)} reshape(bf16[7876352]{0:T(1024)(128)(2,1)} %all-reduce.29.cloned.1.call-done) | data formatting | bytes 31505408 | tf_op jit(solution)/shard_map/all_gather | solution.py:34
  302.7 10.7 fusion.81
  326.4 9.7 reshape_reshape.20
  377.1 8.1 reshape_reshape.21
  410.4 7.9 collective-permute-start.7
  418.3 8.9 collective-permute-start.6
  427.2 9.1 collective-permute-start.5
  436.3 8.9 collective-permute-start.4
  488.1 8.9 collective-permute-start.14
  497.0 8.9 collective-permute-start.13
  505.9 8.9 collective-permute-start.12
  514.8 8.9 collective-permute-start.11
  523.7 8.9 collective-permute-start.9
  538.3 8.0 collective-permute-start.10
  561.8 13.7 convert_reduce_fusion
  649.6 395.9 %fusion.76 = (f32[8,2304]{1,0:T(8,128)S(1)}, f32[8,768]{1,0:T(8,128)S(1)}, f32[8,3072]{1,0:T(8,128)S(1)}, f32[8,512]{1,0:T(8,128)S(1)}) fusion(f32[768,2304]{1,0:T(8,128)} %fusion.69, f32[768,768]{1,0:T(8,128)} %fusion.87, f32[768,3072]{1,0:T(8,128)} %fusion.73, f32[768,512]{1,0:T(8,128)} %fusion.88), kind=kCustom, calls=%all-reduce-scatter.4 | all-reduce-scatter fusion | flops 6815745 | bytes 20660224
  1058.9 8.4 collective-permute-start.138
  1067.3 24.6 %collective-permute-start.137 = (f32[8,512]{1,0:T(8,128)S(1)}, f32[8,512]{1,0:T(8,128)S(1)}, u32[]{:S(2)}, u32[]{:S(2)}) collective-permute-start(f32[8,512]{1,0:T(8,128)S(1)} %get-tuple-element.140), channel_id=1, source_target_pairs={{0,26},{1,27},{2,28},{3,29},{4,30},{5,31},{6,32},{7,33},{8,34},{9,... | collective-permute-start | bytes 49160
  1377.7 67.4 %all-reduce.24 = (f32[768]{0:T(1024)S(1)}, f32[768]{0:T(1024)S(1)}, f32[768]{0:T(1024)S(1)}, f32[768]{0:T(1024)S(1)}, f32[768]{0:T(1024)S(1)}, /*index=5*/f32[76...) all-reduce(f32[768]{0:T(1024)S(1)} %get-tuple-element.114, ...), channel_id=3, replica_groups=mesh['role'=2,'dp'=64] {'role','dp'}, use_global_device_ids=true, to_apply=%region_20.21.clone | all-reduce | flops 12032 | bytes 96256
  1475.4 25.7 %concatenate.18 = f32[262,768]{1,0:T(8,128)S(1)} concatenate(f32[6,768]{1,0:T(8,128)S(1)} %collective-permute-done.79, f32[8,768]{1,0:T(8,128)S(1)} %collective-permute-done.78, f32[8,768]{1,0:T(8,128)} %copy-done.102, f32[8,768]{1,0:T(8,128)} %copy-done.103, f32[8,768]{1,0:T(8,128)} %copy-done.104, f32[8,768]{1,0:T(8,128)} %copy-done.105, f32[8,768]{1,0:T(8,128)} %copy-done.106, ...), dimensions={0} | concatenate | bytes 1609728
  1537.8 32.6 %concatenate.17 = f32[262,2304]{1,0:T(8,128)S(1)} concatenate(f32[6,2304]{1,0:T(8,128)} %copy-done.74, f32[8,2304]{1,0:T(8,128)} %copy-done.71, f32[8,2304]{1,0:T(8,128)} %copy-done.72, f32[8,2304]{1,0:T(8,128)} %copy-done.73, f32[8,2304]{1,0:T(8,128)} %copy-done.75, f32[8,2304]{1,0:T(8,128)} %copy-done.76, f32[8,2304]{1,0:T(8,128)} %copy-done.77, f32[8,2304]{1,0:T(8,128)} %copy-done.78, ...), dimensions={0} | concatenate | bytes 4829184
  1595.2 56.0 %concatenate.19 = f32[262,3072]{1,0:T(8,128)} concatenate(f32[6,3072]{1,0:T(8,128)} %copy-done.41, f32[8,3072]{1,0:T(8,128)S(1)} %collective-permute-done.110, f32[8,3072]{1,0:T(8,128)} %copy-done.42, f32[8,3072]{1,0:T(8,128)} %copy-done.43, f32[8,3072]{1,0:T(8,128)} %copy-done.44, f32[8,3072]{1,0:T(8,128)} %copy-done.45, f32[8,3072]{1,0:T(8,128)} %copy-done.46, ...), dimensions={0} | concatenate | bytes 6438912
  (855 shorter events, 642.6 us)
Async XLA Ops:
  7.2 243.5 %all-reduce.29.cloned.1.call-start = ((), (), s32[]{:S(2)}) async-start(), calls=%async_computation.2 | async-start | bytes 31506432
  32.5 1503.8 %all-reduce.31.cloned.1.call-start = ((), (), s32[]{:S(2)}) async-start(), calls=%async_computation.3 | async-start | bytes 3145728
  400.9 44.3 %collective-permute-start.1 = (bf16[80,512]{1,0:T(8,128)(2,1)S(1)}, bf16[80,512]{1,0:T(8,128)(2,1)S(1)}, u32[]{:S(2)}, u32[]{:S(2)}) collective-permute-start(bf16[80,512]{1,0:T(8,128)(2,1)S(1)} %get-tuple-element.184), channel_id=1, source_target_pairs={{0,1},{1,2},{2,3},{3,4},{4,5},{5,6},{6,7},{7,8},{8,9},{9,10},{10,1... | collective-permute-start | bytes 245768 | tf_op jit(solution)/shard_map/ppermute | solution.py:23
  410.4 56.8 %collective-permute-start.7 = (bf16[80,512]{1,0:T(8,128)(2,1)S(1)}, bf16[80,512]{1,0:T(8,128)(2,1)S(1)}, u32[]{:S(2)}, u32[]{:S(2)}) collective-permute-start(bf16[80,512]{1,0:T(8,128)(2,1)S(1)} %get-tuple-element.178), channel_id=1, source_target_pairs={{0,7},{1,8},{2,9},{3,10},{4,11},{5,12},{6,13},{7,14},{8,15},{9,16}... | collective-permute-start | bytes 245768 | tf_op jit(solution)/shard_map/ppermute | solution.py:23
  418.3 48.8 %collective-permute-start.6 = (bf16[80,512]{1,0:T(8,128)(2,1)S(1)}, bf16[80,512]{1,0:T(8,128)(2,1)S(1)}, u32[]{:S(2)}, u32[]{:S(2)}) collective-permute-start(bf16[80,512]{1,0:T(8,128)(2,1)S(1)} %get-tuple-element.179), channel_id=1, source_target_pairs={{0,6},{1,7},{2,8},{3,9},{4,10},{5,11},{6,12},{7,13},{8,14},{9,15},... | collective-permute-start | bytes 245768 | tf_op jit(solution)/shard_map/ppermute | solution.py:23
  488.1 66.2 %collective-permute-start.14 = (bf16[80,512]{1,0:T(8,128)(2,1)S(1)}, bf16[80,512]{1,0:T(8,128)(2,1)S(1)}, u32[]{:S(2)}, u32[]{:S(2)}) collective-permute-start(bf16[80,512]{1,0:T(8,128)(2,1)S(1)} %get-tuple-element.170), channel_id=1, source_target_pairs={{0,57},{1,58},{2,59},{3,60},{4,61},{5,62},{6,63},{7,0},{8,1},{9,2}... | collective-permute-start | bytes 245768 | tf_op jit(solution)/shard_map/ppermute | solution.py:23
  497.0 56.6 %collective-permute-start.13 = (bf16[80,512]{1,0:T(8,128)(2,1)S(1)}, bf16[80,512]{1,0:T(8,128)(2,1)S(1)}, u32[]{:S(2)}, u32[]{:S(2)}) collective-permute-start(bf16[80,512]{1,0:T(8,128)(2,1)S(1)} %get-tuple-element.171), channel_id=1, source_target_pairs={{0,58},{1,59},{2,60},{3,61},{4,62},{5,63},{6,0},{7,1},{8,2},{9,3},... | collective-permute-start | bytes 245768 | tf_op jit(solution)/shard_map/ppermute | solution.py:23
  505.9 47.1 %collective-permute-start.12 = (bf16[80,512]{1,0:T(8,128)(2,1)S(1)}, bf16[80,512]{1,0:T(8,128)(2,1)S(1)}, u32[]{:S(2)}, u32[]{:S(2)}) collective-permute-start(bf16[80,512]{1,0:T(8,128)(2,1)S(1)} %get-tuple-element.172), channel_id=1, source_target_pairs={{0,59},{1,60},{2,61},{3,62},{4,63},{5,0},{6,1},{7,2},{8,3},{9,4},{... | collective-permute-start | bytes 245768 | tf_op jit(solution)/shard_map/ppermute | solution.py:23
  559.3 1093.5 %reduce-scatter.10.cloned.1.call-start = ((), (), s32[]{:S(2)}) async-start(), calls=%async_computation.1 | async-start | bytes 9510912 | tf_op jit(solution)/shard_map/reduce_scatter | solution.py:344
  1370.9 87.2 %collective-permute-start.104 = (f32[8,3072]{1,0:T(8,128)S(1)}, f32[8,3072]{1,0:T(8,128)S(1)}, u32[]{:S(2)}, u32[]{:S(2)}) collective-permute-start(f32[8,3072]{1,0:T(8,128)S(1)} %get-tuple-element.139), channel_id=1, source_target_pairs={{0,25},{1,26},{2,27},{3,28},{4,29},{5,30},{6,31},{7,32},{8,33},{9,... | collective-permute-start | bytes 294920
  1372.2 88.8 %collective-permute-start.103 = (f32[8,3072]{1,0:T(8,128)S(1)}, f32[8,3072]{1,0:T(8,128)S(1)}, u32[]{:S(2)}, u32[]{:S(2)}) collective-permute-start(f32[8,3072]{1,0:T(8,128)S(1)} %get-tuple-element.139), channel_id=1, source_target_pairs={{0,24},{1,25},{2,26},{3,27},{4,28},{5,29},{6,30},{7,31},{8,32},{9,... | collective-permute-start | bytes 294920
  1373.6 91.9 %collective-permute-start.102 = (f32[8,3072]{1,0:T(8,128)S(1)}, f32[8,3072]{1,0:T(8,128)S(1)}, u32[]{:S(2)}, u32[]{:S(2)}) collective-permute-start(f32[8,3072]{1,0:T(8,128)S(1)} %get-tuple-element.139), channel_id=1, source_target_pairs={{0,23},{1,24},{2,25},{3,26},{4,27},{5,28},{6,29},{7,30},{8,31},{9,... | collective-permute-start | bytes 294920
  1374.9 94.5 %collective-permute-start.101 = (f32[8,3072]{1,0:T(8,128)S(1)}, f32[8,3072]{1,0:T(8,128)S(1)}, u32[]{:S(2)}, u32[]{:S(2)}) collective-permute-start(f32[8,3072]{1,0:T(8,128)S(1)} %get-tuple-element.139), channel_id=1, source_target_pairs={{0,22},{1,23},{2,24},{3,25},{4,26},{5,27},{6,28},{7,29},{8,30},{9,... | collective-permute-start | bytes 294920
  1376.2 95.3 %collective-permute-start.100 = (f32[8,3072]{1,0:T(8,128)S(1)}, f32[8,3072]{1,0:T(8,128)S(1)}, u32[]{:S(2)}, u32[]{:S(2)}) collective-permute-start(f32[8,3072]{1,0:T(8,128)S(1)} %get-tuple-element.139), channel_id=1, source_target_pairs={{0,21},{1,22},{2,23},{3,24},{4,25},{5,26},{6,27},{7,28},{8,29},{9,... | collective-permute-start | bytes 294920
  1458.1 43.0 %collective-permute-start.99 = (f32[8,3072]{1,0:T(8,128)S(1)}, f32[8,3072]{1,0:T(8,128)S(1)}, u32[]{:S(2)}, u32[]{:S(2)}) collective-permute-start(f32[8,3072]{1,0:T(8,128)S(1)} %get-tuple-element.139), channel_id=1, source_target_pairs={{0,20},{1,21},{2,22},{3,23},{4,24},{5,25},{6,26},{7,27},{8,28},{9,... | collective-permute-start | bytes 294920
  1461.0 46.7 %collective-permute-start.98 = (f32[8,3072]{1,0:T(8,128)S(1)}, f32[8,3072]{1,0:T(8,128)S(1)}, u32[]{:S(2)}, u32[]{:S(2)}) collective-permute-start(f32[8,3072]{1,0:T(8,128)S(1)} %get-tuple-element.139), channel_id=1, source_target_pairs={{0,19},{1,20},{2,21},{3,22},{4,23},{5,24},{6,25},{7,26},{8,27},{9,... | collective-permute-start | bytes 294920
  1465.5 45.6 %collective-permute-start.97 = (f32[8,3072]{1,0:T(8,128)S(1)}, f32[8,3072]{1,0:T(8,128)S(1)}, u32[]{:S(2)}, u32[]{:S(2)}) collective-permute-start(f32[8,3072]{1,0:T(8,128)S(1)} %get-tuple-element.139), channel_id=1, source_target_pairs={{0,18},{1,19},{2,20},{3,21},{4,22},{5,23},{6,24},{7,25},{8,26},{9,... | collective-permute-start | bytes 294920
  1469.4 44.2 %collective-permute-start.96 = (f32[8,3072]{1,0:T(8,128)S(1)}, f32[8,3072]{1,0:T(8,128)S(1)}, u32[]{:S(2)}, u32[]{:S(2)}) collective-permute-start(f32[8,3072]{1,0:T(8,128)S(1)} %get-tuple-element.139), channel_id=1, source_target_pairs={{0,17},{1,18},{2,19},{3,20},{4,21},{5,22},{6,23},{7,24},{8,25},{9,... | collective-permute-start | bytes 294920
  1471.5 44.4 %collective-permute-start.95 = (f32[8,3072]{1,0:T(8,128)S(1)}, f32[8,3072]{1,0:T(8,128)S(1)}, u32[]{:S(2)}, u32[]{:S(2)}) collective-permute-start(f32[8,3072]{1,0:T(8,128)S(1)} %get-tuple-element.139), channel_id=1, source_target_pairs={{0,16},{1,17},{2,18},{3,19},{4,20},{5,21},{6,22},{7,23},{8,24},{9,... | collective-permute-start | bytes 294920
  1520.2 50.2 %collective-permute-start.89 = (f32[8,3072]{1,0:T(8,128)S(1)}, f32[8,3072]{1,0:T(8,128)S(1)}, u32[]{:S(2)}, u32[]{:S(2)}) collective-permute-start(f32[8,3072]{1,0:T(8,128)S(1)} %get-tuple-element.139), channel_id=1, source_target_pairs={{0,10},{1,11},{2,12},{3,13},{4,14},{5,15},{6,16},{7,17},{8,18},{9,... | collective-permute-start | bytes 294920
  1524.2 48.3 %collective-permute-start.88 = (f32[8,3072]{1,0:T(8,128)S(1)}, f32[8,3072]{1,0:T(8,128)S(1)}, u32[]{:S(2)}, u32[]{:S(2)}) collective-permute-start(f32[8,3072]{1,0:T(8,128)S(1)} %get-tuple-element.139), channel_id=1, source_target_pairs={{0,9},{1,10},{2,11},{3,12},{4,13},{5,14},{6,15},{7,16},{8,17},{9,1... | collective-permute-start | bytes 294920
  1526.3 49.1 %collective-permute-start.87 = (f32[8,3072]{1,0:T(8,128)S(1)}, f32[8,3072]{1,0:T(8,128)S(1)}, u32[]{:S(2)}, u32[]{:S(2)}) collective-permute-start(f32[8,3072]{1,0:T(8,128)S(1)} %get-tuple-element.139), channel_id=1, source_target_pairs={{0,8},{1,9},{2,10},{3,11},{4,12},{5,13},{6,14},{7,15},{8,16},{9,17... | collective-permute-start | bytes 294920
  1529.0 51.8 %collective-permute-start.86 = (f32[8,3072]{1,0:T(8,128)S(1)}, f32[8,3072]{1,0:T(8,128)S(1)}, u32[]{:S(2)}, u32[]{:S(2)}) collective-permute-start(f32[8,3072]{1,0:T(8,128)S(1)} %get-tuple-element.139), channel_id=1, source_target_pairs={{0,7},{1,8},{2,9},{3,10},{4,11},{5,12},{6,13},{7,14},{8,15},{9,16}... | collective-permute-start | bytes 294920
  1532.2 51.5 %collective-permute-start.85 = (f32[8,3072]{1,0:T(8,128)S(1)}, f32[8,3072]{1,0:T(8,128)S(1)}, u32[]{:S(2)}, u32[]{:S(2)}) collective-permute-start(f32[8,3072]{1,0:T(8,128)S(1)} %get-tuple-element.139), channel_id=1, source_target_pairs={{0,6},{1,7},{2,8},{3,9},{4,10},{5,11},{6,12},{7,13},{8,14},{9,15},... | collective-permute-start | bytes 294920
  (320 other events, 11937.8 us)
Sparse Core Ops, SparseCore 0:
  32.6 218.1 all-reduce.28
  559.4 152.3 all-reduce.30
  717.4 231.5 reduce-scatter.9
where the time goes:
time: 1670 us; the launch traced here: 1660 us
  starting transfers between devices  463 us (28%)
  blocking collectives  463 us (28%)
  local copies, waits for them, and re-layouts  340 us (20%)
  waiting for transfers between devices  246 us (15%)
  matrix products  102 us (6%)
  other arithmetic  26.3 us (2%)
  between operations  19.1 us (1%)
    unnamed x2, blocking collectives  463 us
    unnamed x130, starting transfers between devices  361 us
    unnamed x133, waiting for transfers between devices  222 us
    unnamed x439, local copies, waits for them, and re-layouts  161 us
    ppermute x14, starting transfers between devices, passed_along(): lax.ppermute(array, axis, [(i, (i + by) % count) for i in range(count)])  102 us
    all_gather x1, local copies, waits for them, and re-layouts, gather_together(): lines, at, gathered = (lax.all_gather(line, axis), 0, [])  37.9 us
  transfers between devices with their start and end apart: 147, of which 12 were waited for; matrix products, arithmetic and copies ran while one was open for 40% of the time, Pallas kernels for 0%

commit v1 on v0

v1 whole, which is shorter than its diff:
```python
import jax
import jax.numpy as jnp
from jax import lax
from jax.sharding import Mesh
from jax.sharding import PartitionSpec as P

D = 768
H = 12
HD = 64
FF = 3072
DD = 512
PIX = 768
SIDE = 14
SLOT = 80
IMG_DEV = 8
GRID = 196
N_DP = 64
PART = FF // D

ALL = ("role", "y", "z", "x")

epsilon = 1e-06
masked_score = -1e30

def layer_norm(values, gain, shift):
    average = jnp.mean(values, axis=-1, keepdims=True)
    centered = values - average
    variance = jnp.mean(centered * centered, axis=-1, keepdims=True)
    return centered * lax.rsqrt(variance + epsilon) * gain + shift


def positions():
    quarter = DD // 4
    frequency = 10000.0 ** (-jnp.arange(quarter, dtype=jnp.float32) / quarter)
    places = jnp.arange(GRID, dtype=jnp.int32)
    row_angle = (places // SIDE).astype(jnp.float32)[:, None] * frequency[None, :]
    col_angle = (places % SIDE).astype(jnp.float32)[:, None] * frequency[None, :]
    return jnp.concatenate(
        [jnp.sin(row_angle), jnp.cos(row_angle), jnp.sin(col_angle), jnp.cos(col_angle)], axis=1
    )


def smooth_gate(values):
    return jax.nn.gelu(values, approximate=True)


def transpose_dot(left, right):
    return lax.dot_general(
        left, right, (((0,), (0,)), ((), ())), preferred_element_type=jnp.float32
    )


def dot_right(left, right):
    return lax.dot_general(
        left, right, (((1,), (1,)), ((), ())), preferred_element_type=jnp.float32
    )


def plain_dot(left, right):
    return jnp.dot(left, right, preferred_element_type=jnp.float32)


def column_sum(values):
    return jnp.sum(values.astype(jnp.float32), axis=0)


PAIRS = {
    "high": [(0, 3), (3, 0), (1, 2), (2, 1)],
    "low": [(0, 1), (1, 0), (2, 3), (3, 2)],
}


def halve(state, axis, dim, which):
    at = lax.axis_index(axis)
    bit = at // 2 if which == "high" else at % 2
    half = state.shape[dim] // 2
    kept = lax.dynamic_slice_in_dim(state, bit * half, half, dim)
    sent = lax.dynamic_slice_in_dim(state, (1 - bit) * half, half, dim)
    came = lax.ppermute(sent, axis, PAIRS[which])
    return kept.astype(jnp.float32) + came.astype(jnp.float32)


def scatter_sum(whole, order):
    columns = whole.shape[1]
    role = lax.axis_index("role")
    half = D // 2
    kept = lax.dynamic_slice_in_dim(whole, role * half, half, 0)
    sent = lax.dynamic_slice_in_dim(whole, (1 - role) * half, half, 0)
    came = lax.ppermute(sent, "role", [(0, 1), (1, 0)])
    state = (kept.astype(jnp.float32) + came.astype(jnp.float32)).astype(jnp.bfloat16)
    state = state.reshape(4, 4, 24, columns)
    for axis in order:
        dim = 0 if axis == "y" else 1
        for which in ("high", "low"):
            state = halve(state, axis, dim, which).astype(jnp.bfloat16)
    state = state.reshape(4, 6, columns)
    state = halve(state, "x", 0, "high").astype(jnp.bfloat16)
    return halve(state, "x", 0, "low").reshape(6, columns)


def layer_norm_back(values, gain, upstream):
    average = jnp.mean(values, axis=-1, keepdims=True)
    centered = values - average
    variance = jnp.mean(centered * centered, axis=-1, keepdims=True)
    inverse = lax.rsqrt(variance + epsilon)
    h = centered * inverse
    dh = upstream * gain
    dv = (
        dh
        - jnp.mean(dh, axis=-1, keepdims=True)
        - h * jnp.mean(dh * h, axis=-1, keepdims=True)
    ) * inverse
    lead = tuple(range(values.ndim - 1))
    return dv, jnp.sum(upstream * h, axis=lead), jnp.sum(upstream, axis=lead)


def body(
    patch_rows,
    patch_order,
    visible_count,
    encoded_image,
    first_gain,
    first_shift,
    query_key_value,
    query_bias,
    value_bias,
    output_weight,
    output_bias,
    second_gain,
    second_shift,
    up_weight,
    up_bias,
    down_weight,
    down_bias,
    embed_weight,
    embed_bias,
    mask_token,
    decoder_gain,
    decoder_shift,
    pixel_weight,
    pixel_bias,
    pixel_grad,
):
    device = lax.axis_index(ALL)
    n_dev = 2 * N_DP
    small = jnp.concatenate([embed_bias, mask_token, decoder_gain, decoder_shift])
    small = jnp.pad(small, (0, 2)).reshape(6, 3)
    vectors = jnp.stack(
        [
            first_gain,
            first_shift,
            query_bias,
            value_bias,
            output_bias,
            second_gain,
            second_shift,
            down_bias,
            pixel_bias,
        ],
        axis=1,
    )
    packed = jnp.concatenate(
        [
            query_key_value,
            output_weight,
            up_weight.reshape(6, D, PART).transpose(0, 2, 1).reshape(6, FF),
            down_weight.reshape(6, FF),
            embed_weight,
            pixel_weight.reshape(6, DD),
            vectors,
            up_bias.reshape(6, PART),
            small,
            jnp.zeros((6, 112), jnp.bfloat16),
        ],
        axis=1,
    )
    whole = lax.all_gather(packed, "x", tiled=True)
    whole = lax.all_gather(whole, ("role", "y", "z"), tiled=True)
    at = 0

    def take(width):
        nonlocal at
        at += width
        return whole[:, at - width : at]

    mix_weight = take(3 * D)
    out_weight = take(D)
    hidden_weight = take(FF)
    back_weight = jnp.concatenate([take(D) for _ in range(PART)], axis=0)
    emb_weight = take(DD)
    pix_weight = take(DD).reshape(DD, PIX)
    rest = take(128)[:, :16].astype(jnp.float32)
    rows = rest.T
    gain_one, shift_one, bias_query, bias_value, out_bias, gain_two, shift_two, back_bias, pix_bias = (
        rows[k] for k in range(9)
    )
    hidden_bias = rows[9:13].reshape(FF)
    fours = rest[:, 13:16].reshape(n_dev, 18)[:, :16].reshape(n_dev, 4, 4)
    fours = fours.transpose(1, 0, 2).reshape(4, DD)
    emb_bias, token_mask, gain_three, shift_three = (fours[k] for k in range(4))

    row_count = IMG_DEV * SLOT
    image_count = encoded_image.shape[0]
    scale = HD ** (-0.5)
    held = lax.dynamic_slice_in_dim(encoded_image, device * IMG_DEV, IMG_DEV)
    held_count = visible_count[held]
    held_order = patch_order[held][:, :SLOT]
    live_slot = jnp.arange(SLOT, dtype=jnp.int32)[None, :] < held_count[:, None]

    own_images = device * IMG_DEV + jnp.arange(IMG_DEV, dtype=jnp.int32)
    found = encoded_image[None, :] == own_images[:, None]
    source_slot = jnp.sum(
        jnp.where(found, jnp.arange(image_count, dtype=jnp.int32)[None, :], 0), axis=1
    )
    source_place = source_slot % IMG_DEV
    image_of = jnp.sum(
        jnp.where(
            source_place[None, :] == jnp.arange(IMG_DEV, dtype=jnp.int32)[:, None],
            jnp.arange(IMG_DEV, dtype=jnp.int32)[None, :],
            0,
        ),
        axis=1,
    )

    def across(step):
        return [
            (r * N_DP + p, (1 - r) * N_DP + (p + step) % N_DP) for r in range(2) for p in range(N_DP)
        ]

    upstream = jnp.stack(
        [
            lax.ppermute(
                lax.dynamic_index_in_dim(pixel_grad, image_of[s], 0, keepdims=False), ALL, across(-s)
            )
            for s in range(IMG_DEV)
        ]
    )

    shape_four = (IMG_DEV, SLOT, H, HD)
    inputs = patch_rows.astype(jnp.float32)
    normed_low = layer_norm(inputs, gain_one, shift_one).astype(jnp.bfloat16)
    bias_mix = jnp.concatenate([bias_query, jnp.zeros((D,), jnp.float32), bias_value])
    mixed = (plain_dot(normed_low, mix_weight) + bias_mix).astype(jnp.bfloat16)
    queries = mixed[:, :D].reshape(shape_four)
    keys_all = mixed[:, D : 2 * D].reshape(shape_four)
    values_all = mixed[:, 2 * D :].reshape(shape_four)
    raw_scores = (
        jnp.einsum("sqhe,skhe->shqk", queries, keys_all, preferred_element_type=jnp.float32) * scale
    )
    scores = jnp.where(live_slot[:, None, None, :], raw_scores, masked_score)
    probs = jax.nn.softmax(scores, axis=-1)
    probs_low = probs.astype(jnp.bfloat16)
    attended = (
        jnp.einsum("shqk,skhe->sqhe", probs_low, values_all, preferred_element_type=jnp.float32)
        .reshape(row_count, D)
        .astype(jnp.bfloat16)
    )
    resid = inputs + (plain_dot(attended, out_weight) + out_bias)
    normed_two_low = layer_norm(resid, gain_two, shift_two).astype(jnp.bfloat16)
    hidden = plain_dot(normed_two_low, hidden_weight) + hidden_bias
    active_low = smooth_gate(hidden).astype(jnp.bfloat16)
    encoded = resid + (plain_dot(active_low, back_weight) + back_bias)
    encoded_low = encoded.astype(jnp.bfloat16)
    embedded = (plain_dot(encoded_low, emb_weight) + emb_bias).astype(jnp.bfloat16)
    blocks = embedded.reshape(IMG_DEV, SLOT, DD)
    placement = (
        held_order[:, None, :] == jnp.arange(GRID, dtype=jnp.int32)[None, :, None]
    ) & live_slot[:, None, :]
    place_low = placement.astype(jnp.bfloat16)
    masked_share = 1.0 - jnp.sum(placement.astype(jnp.float32), axis=2)
    grid = (
        jnp.einsum("pgt,ptc->pgc", place_low, blocks, preferred_element_type=jnp.float32)
        + masked_share[..., None] * token_mask
        + positions()[None]
    )
    decoded_low = layer_norm(grid, gain_three, shift_three).astype(jnp.bfloat16)
    pixels_held = (
        jnp.einsum("pgc,cx->pgx", decoded_low, pix_weight, preferred_element_type=jnp.float32)
        + pix_bias
    ).astype(jnp.bfloat16)
    pixels = jnp.zeros((IMG_DEV, GRID, PIX), jnp.bfloat16)
    for s in range(IMG_DEV):
        came = lax.ppermute(pixels_held[s], ALL, across(s))
        pixels = lax.dynamic_update_index_in_dim(pixels, came, image_of[s], 0)

    grad_pixel_weight = jnp.einsum(
        "pgc,pgx->cx", decoded_low, upstream, preferred_element_type=jnp.float32
    )
    grad_pixel_bias = jnp.sum(upstream.astype(jnp.float32), axis=(0, 1))
    grad_decoded = jnp.einsum(
        "pgx,cx->pgc", upstream, pix_weight, preferred_element_type=jnp.float32
    )
    grad_grid, grad_decoder_gain, grad_decoder_shift = layer_norm_back(grid, gain_three, grad_decoded)
    grad_mask_token = jnp.sum(masked_share[..., None] * grad_grid, axis=(0, 1))
    grad_embedded = (
        jnp.einsum(
            "pgt,pgc->ptc",
            place_low,
            grad_grid.astype(jnp.bfloat16),
            preferred_element_type=jnp.float32,
        )
        .astype(jnp.bfloat16)
        .reshape(row_count, DD)
    )
    grad_embed_weight = transpose_dot(encoded_low, grad_embedded)
    grad_embed_bias = column_sum(grad_embedded)
    grad_encoded = dot_right(grad_embedded, emb_weight)
    grad_branch_two = grad_encoded.astype(jnp.bfloat16)
    grad_down_weight = [
        transpose_dot(active_low[:, j * D : (j + 1) * D], grad_branch_two) for j in range(PART)
    ]
    group_one = jnp.concatenate(
        [
            g.astype(jnp.bfloat16)
            for g in grad_down_weight + [grad_embed_weight, grad_pixel_weight.reshape(D, DD)]
        ],
        axis=1,
    )
    shard_one = scatter_sum(group_one, "yz")
    grad_down_bias = column_sum(grad_branch_two)
    grad_active = dot_right(grad_branch_two, back_weight)
    gate_back = jax.vjp(smooth_gate, hidden)[1]
    grad_hidden = gate_back(grad_active)[0].astype(jnp.bfloat16)
    grad_up_weight = transpose_dot(normed_two_low, grad_hidden)
    grad_up_bias = column_sum(grad_hidden)
    grad_normed_two = dot_right(grad_hidden, hidden_weight)
    grad_resid_part, grad_second_gain, grad_second_shift = layer_norm_back(
        resid, gain_two, grad_normed_two
    )
    grad_resid = grad_encoded + grad_resid_part
    grad_branch = grad_resid.astype(jnp.bfloat16)
    grad_output_weight = transpose_dot(attended, grad_branch)
    group_two = jnp.concatenate(
        [grad_up_weight.astype(jnp.bfloat16), grad_output_weight.astype(jnp.bfloat16)], axis=1
    )
    shard_two = scatter_sum(group_two, "zy")
    grad_output_bias = column_sum(grad_branch)
    grad_attended = dot_right(grad_branch, out_weight).astype(jnp.bfloat16).reshape(shape_four)
    grad_probs = jnp.einsum(
        "sqhe,skhe->shqk", grad_attended, values_all, preferred_element_type=jnp.float32
    )
    grad_values = jnp.einsum(
        "shqk,sqhe->skhe", probs_low, grad_attended, preferred_element_type=jnp.float32
    )
    grad_scores = (
        probs * (grad_probs - jnp.sum(probs * grad_probs, axis=-1, keepdims=True))
    ).astype(jnp.bfloat16)
    grad_queries = (
        jnp.einsum("shqk,skhe->sqhe", grad_scores, keys_all, preferred_element_type=jnp.float32)
        * scale
    )
    grad_keys = (
        jnp.einsum("shqk,sqhe->skhe", grad_scores, queries, preferred_element_type=jnp.float32)
        * scale
    )
    grad_mixed = jnp.concatenate(
        [
            grad_queries.reshape(row_count, D),
            grad_keys.reshape(row_count, D),
            grad_values.reshape(row_count, D),
        ],
        axis=1,
    ).astype(jnp.bfloat16)
    grad_mix_weight = transpose_dot(normed_low, grad_mixed)
    grad_query_bias = column_sum(grad_mixed[:, :D])
    grad_value_bias = column_sum(grad_mixed[:, 2 * D :])
    grad_normed = dot_right(grad_mixed, mix_weight)
    grad_input_part, grad_first_gain, grad_first_shift = layer_norm_back(
        inputs, gain_one, grad_normed
    )
    patch_grad = (grad_resid + grad_input_part).astype(jnp.bfloat16)
    nines = jnp.stack(
        [
            grad_first_gain,
            grad_first_shift,
            grad_query_bias,
            grad_value_bias,
            grad_output_bias,
            grad_second_gain,
            grad_second_shift,
            grad_down_bias,
            grad_pixel_bias,
        ]
    )
    fours = jnp.stack([grad_embed_bias, grad_mask_token, grad_decoder_gain, grad_decoder_shift])
    fours = fours.reshape(4, n_dev, 4).transpose(1, 0, 2).reshape(n_dev, 16)
    fours = jnp.pad(fours, ((0, 0), (0, 2))).reshape(D, 3)
    rows = jnp.concatenate([nines, grad_up_bias.reshape(PART, D)]).T
    group_three = jnp.concatenate(
        [
            grad_mix_weight.astype(jnp.bfloat16),
            rows.astype(jnp.bfloat16),
            fours.astype(jnp.bfloat16),
            jnp.zeros((D, 112), jnp.bfloat16),
        ],
        axis=1,
    )
    shard_three = scatter_sum(group_three, "yz")
    vec = shard_three[:, 3 * D :]
    tail = vec[:, 13:16].reshape(18)
    return (
        pixels,
        patch_grad,
        vec[:, 0],
        vec[:, 1],
        shard_three[:, : 3 * D],
        vec[:, 2],
        vec[:, 3],
        shard_two[:, FF:],
        vec[:, 4],
        vec[:, 5],
        vec[:, 6],
        shard_two[:, :FF].reshape(6, PART, D).transpose(0, 2, 1).reshape(6, FF),
        vec[:, 9:13].reshape(6 * PART),
        shard_one[:, :FF].reshape(6 * PART, D),
        vec[:, 7],
        shard_one[:, FF : FF + DD],
        tail[0:4],
        tail[4:8],
        tail[8:12],
        tail[12:16],
        shard_one[:, FF + DD :].reshape(4, PIX),
        vec[:, 8],
    )


def solution(mesh):
    mesh = Mesh(mesh.devices.reshape(2, 4, 4, 4), ALL)
    two, one = P(ALL, None), P(ALL)
    placed = (two, P(), P(), P(), one, one, two, one, one, two, one, one, one, two, one, two, one)
    placed += (two, one, one, one, one, two, one, P(ALL, None, None))
    given = (P(ALL, None, None), two, one, one, two, one, one, two, one, one, one, two, one, two, one)
    given += (two, one, one, one, one, two, one)
    return jax.shard_map(body, mesh=mesh, in_specs=placed, out_specs=given, check_vma=False)
```

time: 1670 us -> 671 us (0.40)
  blocking collectives: 463 us -> 13.4 us
  starting transfers between devices: 463 us -> 83.1 us
  waiting for transfers between devices: 246 us -> 132 us
  local copies, waits for them, and re-layouts: 340 us -> 254 us
    unnamed x2 -> x0, blocking collectives: 463 us -> none
    unnamed x130 -> x0, starting transfers between devices: 361 us -> none
    unnamed x133 -> x1, waiting for transfers between devices: 222 us -> 0.02 us
    unnamed x439 -> x197, local copies, waits for them, and re-layouts: 161 us -> 28.9 us
    dynamic_update_slice x0 -> x8, local copies, waits for them, and re-layouts: none -> 94.4 us  [body(): pixels = lax.dynamic_update_index_in_dim(pixels, came, image_of[s], 0)]
    ppermute x16 -> x37, waiting for transfers between devices: 24.5 us -> 113 us  [the longest x18 82.5 us: halve(): came = lax.ppermute(sent, axis, PAIRS[which])]
    all_gather x1 -> x0, local copies, waits for them, and re-layouts: 37.9 us -> none  [gather_together(): lines, at, gathered = (lax.all_gather(line, axis), 0, [])]
    ppermute x16 -> x37, starting transfers between devices: 102 us -> 83 us  [the longest x8 42.4 us: body(): came = lax.ppermute(pixels_held[s], ALL, across(s))]
  transfers between devices with their start and end apart: 147 -> 38, of which waited for: 12 -> 18; matrix products, arithmetic and copies ran while one was open for 40% -> 29% of each run, Pallas kernels for 0% -> 0%
where the time goes in v1:
time: 671 us; the launch traced here: 659 us
  local copies, waits for them, and re-layouts  254 us (38%)
  waiting for transfers between devices  132 us (20%)
  matrix products  109 us (16%)
  starting transfers between devices  83.1 us (12%)
  other arithmetic  35.9 us (5%)
  between operations  31.5 us (5%)
  blocking collectives  13.4 us (2%)
    dynamic_update_slice x8, local copies, waits for them, and re-layouts, body(): pixels = lax.dynamic_update_index_in_dim(pixels, came, image_of[s], 0)  94.4 us
    ppermute x18, waiting for transfers between devices, halve(): came = lax.ppermute(sent, axis, PAIRS[which])  82.5 us
    ppermute x8, starting transfers between devices, body(): came = lax.ppermute(pixels_held[s], ALL, across(s))  42.4 us
    dot_general x5, matrix products, dot_right(): lax.dot_general(left, right, (((1,), (1,)), ((), ())), preferred_element_...  33.3 us
    unnamed x197, local copies, waits for them, and re-layouts  28.9 us
    ppermute x18, starting transfers between devices, halve(): came = lax.ppermute(sent, axis, PAIRS[which])  24.4 us
    dot_general x5, matrix products, plain_dot(): return jnp.dot(left, right, preferred_element_type=jnp.float32)  23.4 us
    dot_general x8, matrix products, transpose_dot(): lax.dot_general(left, right, (((0,), (0,)), ((), ())), preferred_element_...  19 us
  transfers between devices with their start and end apart: 38, of which 18 were waited for; matrix products, arithmetic and copies ran while one was open for 29% of the time, Pallas kernels for 0%

profile of v1, /device:TPU:8, one launch (start us, length us, event | category | flops | bytes accessed | tf_op | source)
XLA Modules:
  0.0 658.7 jit_solution(2042530649263606989)
XLA Ops:
  24.3 13.4 %all-gather = bf16[4,6,10368]{2,1,0:T(8,128)(2,1)S(1)} all-gather(bf16[1,6,10368]{2,1,0:T(8,128)(2,1)S(1)} %bitcast.187), channel_id=1, replica_groups=mesh['role'=2,'y'=4,'z'=4,'x'=4] {'x'}, dimensions={0}, use_global_device_ids=true | all-gather | bytes 622080 | tf_op jit(solution)/shard_map/all_gather | solution.py:177
  62.7 6.6 %collective-permute-start.9 = (bf16[196,768]{1,0:T(8,128)(2,1)}, bf16[196,768]{1,0:T(8,128)(2,1)}, u32[]{:S(2)}, u32[]{:S(2)}) collective-permute-start(bf16[196,768]{1,0:T(8,128)(2,1)} %bitcast.169), channel_id=1, source_target_pairs={{0,127},{1,64},{2,65},{3,66},{4,67},{5,68},{6,69},{7,70},{8,71},{9... | collective-permute-start | bytes 903176 | tf_op jit(solution)/shard_map/ppermute | solution.py:232
  96.1 8.0 %collective-permute-done.13 = bf16[196,768]{1,0:T(8,128)(2,1)S(1)} collective-permute-done((bf16[196,768]{1,0:T(8,128)(2,1)}, bf16[196,768]{1,0:T(8,128)(2,1)S(1)}, u32[]{:S(2)}, u32[]{:S(2)}) %collective-permute-start.13) | collective-permute-done | bytes 301088 | tf_op jit(solution)/shard_map/ppermute | solution.py:232
  116.8 18.8 %all-gather.3.cloned.1.call-done = bf16[768,10368]{1,0:T(8,128)(2,1)} async-done(((bf16[24,10368]{1,0:T(8,128)(2,1)}), bf16[768,10368]{1,0:T(8,128)(2,1)}) %all-gather.3.cloned.1.call-update) | async-done | bytes 15925264 | tf_op jit(solution)/shard_map/all_gather | solution.py:178
  188.5 11.6 %multiply_convert_fusion = (bf16[640,3072]{1,0:T(8,128)(2,1)S(1)}, f32[640,3072]{1,0:T(8,128)}) fusion(f32[3072]{0:T(1024)S(1)} %copy-done.64, bf16[768,10368]{1,0:T(8,128)(2,1)} %all-gather.3.cloned.1.call-done, f32[640,768]{1,0:T(8,128)S(1)} %get-tuple-element.109, f32[768]{0:T(1024)S(1)} %copy-done.73, f32[768]{0:T(1024)S(1)} %copy-done.56, ...), kind=kOutput, calls=%fused_computation.12 | convolution fusion | flops 3042017280 | bytes 18504704 | tf_op jit(solution)/shard_map/dot_general | solution.py:60
  219.1 17.2 %fusion.98 = (bf16[3072]{0:T(1024)(128)(2,1)S(1)}, bf16[640,3072]{1,0:T(8,128)(2,1)S(1)}) fusion(f32[640,3072]{1,0:T(8,128)} %get-tuple-element.111, f32[3072]{0:T(1024)S(1)} %copy-done.64, bf16[640,768]{1,0:T(8,128)(2,1)S(1)} %get-tuple-element.54, bf16[768,768]{1,0:T(8,128)(2,1)S(1)} %copy-done.31, bf16[768,768]{1,0:T(8,128)(2,1)S(1)} %copy-done.33, ...), kind=kOutput, calls=%fused_computation.284 | convolution fusion | flops 3082023936 | bytes 17516544 | tf_op jit(solution)/shard_map/dot_general | solution.py:54
  236.3 6.5 convolution_convert_fusion
  314.8 6.5 concatenate.41
  328.8 16.9 %collective-permute-start.7 = (bf16[196,768]{1,0:T(8,128)(2,1)}, bf16[196,768]{1,0:T(8,128)(2,1)S(1)}, u32[]{:S(2)}, u32[]{:S(2)}) collective-permute-start(bf16[196,768]{1,0:T(8,128)(2,1)} %get-tuple-element.66), channel_id=1, source_target_pairs={{0,71},{1,72},{2,73},{3,74},{4,75},{5,76},{6,77},{7,78},{8,79},{9,... | collective-permute-start | bytes 903176 | tf_op jit(solution)/shard_map/ppermute | solution.py:283
  365.9 16.4 %collective-permute-done.17 = bf16[2,4,24,2432]{3,2,1,0:T(8,128)(2,1)S(1)} collective-permute-done((bf16[2,4,24,2432]{3,2,1,0:T(8,128)(2,1)S(1)}, bf16[2,4,24,2432]{3,2,1,0:T(8,128)(2,1)S(1)}, u32[]{:S(2)}, u32[]{:S(2)}) %collective-permute-start.17) | collective-permute-done | bytes 933920 | tf_op jit(solution)/shard_map/ppermute | solution.py:79
  392.1 13.5 %collective-permute-done.4 = bf16[196,768]{1,0:T(8,128)(2,1)S(1)} collective-permute-done((bf16[196,768]{1,0:T(8,128)(2,1)S(1)}, bf16[196,768]{1,0:T(8,128)(2,1)S(1)}, u32[]{:S(2)}, u32[]{:S(2)}) %collective-permute-start.4) | collective-permute-done | bytes 301088 | tf_op jit(solution)/shard_map/ppermute | solution.py:283
  405.6 14.8 %collective-permute-start.1 = (bf16[196,768]{1,0:T(8,128)(2,1)S(1)}, bf16[196,768]{1,0:T(8,128)(2,1)S(1)}, u32[]{:S(2)}, u32[]{:S(2)}) collective-permute-start(bf16[196,768]{1,0:T(8,128)(2,1)S(1)} %copy-done.44), channel_id=1, source_target_pairs={{0,65},{1,66},{2,67},{3,68},{4,69},{5,70},{6,71},{7,72},{8,73},{9,... | collective-permute-start | bytes 903176 | tf_op jit(solution)/shard_map/ppermute | solution.py:283
  439.7 11.8 %dynamic_update_slice.25 = bf16[8,196,768]{2,0,1:T(8,128)(2,1)} dynamic-update-slice(bf16[8,196,768]{2,0,1:T(8,128)(2,1)} %broadcast_in_dim.71, bf16[1,196,768]{2,0,1:T(2,128)(2,1)} %copy.306, s32[]{:T(128)S(6)} %select_n.207, s32[]{:T(128)} %constant.204.clone.1, s32[]{:T(128)} %constant.204.clone.1) | dynamic-update-slice | bytes 602116 | tf_op jit(solution)/shard_map/jit(dynamic_update_index_in_dim)/dynamic_update_slice | solution.py:284
  451.5 11.8 %dynamic_update_slice.26 = bf16[8,196,768]{2,0,1:T(8,128)(2,1)} dynamic-update-slice(bf16[8,196,768]{2,0,1:T(8,128)(2,1)} %dynamic_update_slice.25, bf16[1,196,768]{2,0,1:T(2,128)(2,1)} %copy.307, s32[]{:T(128)S(6)} %select_n.208, s32[]{:T(128)} %constant.204.clone.1, s32[]{:T(128)} %constant.204.clone.1) | dynamic-update-slice | bytes 602116 | tf_op jit(solution)/shard_map/jit(dynamic_update_index_in_dim)/dynamic_update_slice | solution.py:284
  463.3 11.8 %dynamic_update_slice.27 = bf16[8,196,768]{2,0,1:T(8,128)(2,1)} dynamic-update-slice(bf16[8,196,768]{2,0,1:T(8,128)(2,1)} %dynamic_update_slice.26, bf16[1,196,768]{2,0,1:T(2,128)(2,1)} %copy.308, s32[]{:T(128)S(6)} %select_n.209, s32[]{:T(128)} %constant.204.clone.1, s32[]{:T(128)} %constant.204.clone.1) | dynamic-update-slice | bytes 602116 | tf_op jit(solution)/shard_map/jit(dynamic_update_index_in_dim)/dynamic_update_slice | solution.py:284
  475.1 11.8 %dynamic_update_slice.28 = bf16[8,196,768]{2,0,1:T(8,128)(2,1)} dynamic-update-slice(bf16[8,196,768]{2,0,1:T(8,128)(2,1)} %dynamic_update_slice.27, bf16[1,196,768]{2,0,1:T(2,128)(2,1)} %copy.309, s32[]{:T(128)S(6)} %select_n.210, s32[]{:T(128)} %constant.204.clone.1, s32[]{:T(128)} %constant.204.clone.1) | dynamic-update-slice | bytes 602116 | tf_op jit(solution)/shard_map/jit(dynamic_update_index_in_dim)/dynamic_update_slice | solution.py:284
  486.9 11.8 %dynamic_update_slice.29 = bf16[8,196,768]{2,0,1:T(8,128)(2,1)} dynamic-update-slice(bf16[8,196,768]{2,0,1:T(8,128)(2,1)} %dynamic_update_slice.28, bf16[1,196,768]{2,0,1:T(2,128)(2,1)} %copy.310, s32[]{:T(128)S(6)} %select_n.211, s32[]{:T(128)} %constant.204.clone.1, s32[]{:T(128)} %constant.204.clone.1) | dynamic-update-slice | bytes 602116 | tf_op jit(solution)/shard_map/jit(dynamic_update_index_in_dim)/dynamic_update_slice | solution.py:284
  498.7 11.8 %dynamic_update_slice.30 = bf16[8,196,768]{2,0,1:T(8,128)(2,1)} dynamic-update-slice(bf16[8,196,768]{2,0,1:T(8,128)(2,1)} %dynamic_update_slice.29, bf16[1,196,768]{2,0,1:T(2,128)(2,1)} %copy.311, s32[]{:T(128)S(6)} %select_n.212, s32[]{:T(128)} %constant.204.clone.1, s32[]{:T(128)} %constant.204.clone.1) | dynamic-update-slice | bytes 602116 | tf_op jit(solution)/shard_map/jit(dynamic_update_index_in_dim)/dynamic_update_slice | solution.py:284
  510.5 11.8 %dynamic_update_slice.31 = bf16[8,196,768]{2,0,1:T(8,128)(2,1)} dynamic-update-slice(bf16[8,196,768]{2,0,1:T(8,128)(2,1)} %dynamic_update_slice.30, bf16[1,196,768]{2,0,1:T(2,128)(2,1)} %copy.312, s32[]{:T(128)S(6)} %select_n.213, s32[]{:T(128)} %constant.204.clone.1, s32[]{:T(128)} %constant.204.clone.1) | dynamic-update-slice | bytes 602116 | tf_op jit(solution)/shard_map/jit(dynamic_update_index_in_dim)/dynamic_update_slice | solution.py:284
  522.3 11.8 %dynamic_update_slice.32 = bf16[8,196,768]{2,0,1:T(8,128)(2,1)} dynamic-update-slice(bf16[8,196,768]{2,0,1:T(8,128)(2,1)} %dynamic_update_slice.31, bf16[1,196,768]{2,0,1:T(2,128)(2,1)S(1)} %copy.313, s32[]{:T(128)S(6)} %select_n.214, s32[]{:T(128)} %constant.204.clone.1, s32[]{:T(128)} %constant.204.clone.1) | dynamic-update-slice | bytes 602116 | tf_op jit(solution)/shard_map/jit(dynamic_update_index_in_dim)/dynamic_update_slice | solution.py:284
  565.4 16.1 %collective-permute-done.24 = bf16[4,2,24,3840]{3,2,1,0:T(8,128)(2,1)} collective-permute-done((bf16[4,2,24,3840]{3,2,1,0:T(8,128)(2,1)}, bf16[4,2,24,3840]{3,2,1,0:T(8,128)(2,1)}, u32[]{:S(2)}, u32[]{:S(2)}) %collective-permute-start.24) | collective-permute-done | bytes 1474592 | tf_op jit(solution)/shard_map/ppermute | solution.py:79
  584.3 10.7 %collective-permute-done.31 = bf16[2,4,24,4096]{3,2,1,0:T(8,128)(2,1)} collective-permute-done((bf16[2,4,24,4096]{3,2,1,0:T(8,128)(2,1)}, bf16[2,4,24,4096]{3,2,1,0:T(8,128)(2,1)}, u32[]{:S(2)}, u32[]{:S(2)}) %collective-permute-start.31) | collective-permute-done | bytes 1572896 | tf_op jit(solution)/shard_map/ppermute | solution.py:79
  597.0 8.6 %collective-permute-start.32 = (bf16[1,4,24,4096]{3,2,1,0:T(8,128)(2,1)S(1)}, bf16[1,4,24,4096]{3,2,1,0:T(8,128)(2,1)S(1)}, u32[]{:S(2)}, u32[]{:S(2)}) collective-permute-start(bf16[1,4,24,4096]{3,2,1,0:T(8,128)(2,1)S(1)} %constant_dynamic-slice_fusion.3), channel_id=1, source_target_pairs={{0,16},{16,0},{32,48},{48,32},{1,17},{17,1},{33,49},{49,33},{2,18}... | collective-permute-start | bytes 2359304 | tf_op jit(solution)/shard_map/ppermute | solution.py:79
  605.9 15.4 %collective-permute-done.32 = bf16[1,4,24,4096]{3,2,1,0:T(8,128)(2,1)S(1)} collective-permute-done((bf16[1,4,24,4096]{3,2,1,0:T(8,128)(2,1)S(1)}, bf16[1,4,24,4096]{3,2,1,0:T(8,128)(2,1)S(1)}, u32[]{:S(2)}, u32[]{:S(2)}) %collective-permute-start.32) | collective-permute-done | bytes 786464 | tf_op jit(solution)/shard_map/ppermute | solution.py:79
  (496 shorter events, 331.7 us)
Async XLA Ops:
  7.2 128.4 %all-gather.3.cloned.1.call-start = ((), (), s32[]{:S(2)}) async-start(), calls=%async_computation | async-start | bytes 16422912 | tf_op jit(solution)/shard_map/all_gather | solution.py:178
  61.9 19.6 %collective-permute-start.8 = (bf16[196,768]{1,0:T(8,128)(2,1)}, bf16[196,768]{1,0:T(8,128)(2,1)S(1)}, u32[]{:S(2)}, u32[]{:S(2)}) collective-permute-start(bf16[196,768]{1,0:T(8,128)(2,1)} %bitcast.170), channel_id=1, source_target_pairs={{0,64},{1,65},{2,66},{3,67},{4,68},{5,69},{6,70},{7,71},{8,72},{9,... | collective-permute-start | bytes 903176 | tf_op jit(solution)/shard_map/ppermute | solution.py:232
  62.7 23.0 %collective-permute-start.9 = (bf16[196,768]{1,0:T(8,128)(2,1)}, bf16[196,768]{1,0:T(8,128)(2,1)}, u32[]{:S(2)}, u32[]{:S(2)}) collective-permute-start(bf16[196,768]{1,0:T(8,128)(2,1)} %bitcast.169), channel_id=1, source_target_pairs={{0,127},{1,64},{2,65},{3,66},{4,67},{5,68},{6,69},{7,70},{8,71},{9... | collective-permute-start | bytes 903176 | tf_op jit(solution)/shard_map/ppermute | solution.py:232
  70.0 20.6 %collective-permute-start.10 = (bf16[196,768]{1,0:T(8,128)(2,1)}, bf16[196,768]{1,0:T(8,128)(2,1)}, u32[]{:S(2)}, u32[]{:S(2)}) collective-permute-start(bf16[196,768]{1,0:T(8,128)(2,1)} %bitcast.168), channel_id=1, source_target_pairs={{0,126},{1,127},{2,64},{3,65},{4,66},{5,67},{6,68},{7,69},{8,70},{... | collective-permute-start | bytes 903176 | tf_op jit(solution)/shard_map/ppermute | solution.py:232
  71.3 22.7 %collective-permute-start.11 = (bf16[196,768]{1,0:T(8,128)(2,1)}, bf16[196,768]{1,0:T(8,128)(2,1)}, u32[]{:S(2)}, u32[]{:S(2)}) collective-permute-start(bf16[196,768]{1,0:T(8,128)(2,1)} %bitcast.167), channel_id=1, source_target_pairs={{0,125},{1,126},{2,127},{3,64},{4,65},{5,66},{6,67},{7,68},{8,69},... | collective-permute-start | bytes 903176 | tf_op jit(solution)/shard_map/ppermute | solution.py:232
  72.0 23.0 %collective-permute-start.12 = (bf16[196,768]{1,0:T(8,128)(2,1)}, bf16[196,768]{1,0:T(8,128)(2,1)}, u32[]{:S(2)}, u32[]{:S(2)}) collective-permute-start(bf16[196,768]{1,0:T(8,128)(2,1)} %bitcast.166), channel_id=1, source_target_pairs={{0,124},{1,125},{2,126},{3,127},{4,64},{5,65},{6,66},{7,67},{8,68}... | collective-permute-start | bytes 903176 | tf_op jit(solution)/shard_map/ppermute | solution.py:232
  81.6 22.5 %collective-permute-start.13 = (bf16[196,768]{1,0:T(8,128)(2,1)}, bf16[196,768]{1,0:T(8,128)(2,1)S(1)}, u32[]{:S(2)}, u32[]{:S(2)}) collective-permute-start(bf16[196,768]{1,0:T(8,128)(2,1)} %bitcast.165), channel_id=1, source_target_pairs={{0,123},{1,124},{2,125},{3,126},{4,127},{5,64},{6,65},{7,66},{8,67... | collective-permute-start | bytes 903176 | tf_op jit(solution)/shard_map/ppermute | solution.py:232
  85.7 18.5 %collective-permute-start.14 = (bf16[196,768]{1,0:T(8,128)(2,1)}, bf16[196,768]{1,0:T(8,128)(2,1)S(1)}, u32[]{:S(2)}, u32[]{:S(2)}) collective-permute-start(bf16[196,768]{1,0:T(8,128)(2,1)} %bitcast.164), channel_id=1, source_target_pairs={{0,122},{1,123},{2,124},{3,125},{4,126},{5,127},{6,64},{7,65},{8,6... | collective-permute-start | bytes 903176 | tf_op jit(solution)/shard_map/ppermute | solution.py:232
  324.3 32.1 %collective-permute-start.16 = (bf16[384,2432]{1,0:T(8,128)(2,1)}, bf16[384,2432]{1,0:T(8,128)(2,1)}, u32[]{:S(2)}, u32[]{:S(2)}) collective-permute-start(bf16[384,2432]{1,0:T(8,128)(2,1)} %constant_dynamic-slice_fusion.18), channel_id=1, source_target_pairs={{0,64},{64,0},{1,65},{65,1},{2,66},{66,2},{3,67},{67,3},{4,68},{68... | collective-permute-start | bytes 5603336 | tf_op jit(solution)/shard_map/ppermute | solution.py:89
  328.8 56.6 %collective-permute-start.7 = (bf16[196,768]{1,0:T(8,128)(2,1)}, bf16[196,768]{1,0:T(8,128)(2,1)S(1)}, u32[]{:S(2)}, u32[]{:S(2)}) collective-permute-start(bf16[196,768]{1,0:T(8,128)(2,1)} %get-tuple-element.66), channel_id=1, source_target_pairs={{0,71},{1,72},{2,73},{3,74},{4,75},{5,76},{6,77},{7,78},{8,79},{9,... | collective-permute-start | bytes 903176 | tf_op jit(solution)/shard_map/ppermute | solution.py:283
  345.7 44.9 %collective-permute-start.6 = (bf16[196,768]{1,0:T(8,128)(2,1)}, bf16[196,768]{1,0:T(8,128)(2,1)S(1)}, u32[]{:S(2)}, u32[]{:S(2)}) collective-permute-start(bf16[196,768]{1,0:T(8,128)(2,1)} %get-tuple-element.67), channel_id=1, source_target_pairs={{0,70},{1,71},{2,72},{3,73},{4,74},{5,75},{6,76},{7,77},{8,78},{9,... | collective-permute-start | bytes 903176 | tf_op jit(solution)/shard_map/ppermute | solution.py:283
  345.7 46.1 %collective-permute-start.5 = (bf16[196,768]{1,0:T(8,128)(2,1)}, bf16[196,768]{1,0:T(8,128)(2,1)S(1)}, u32[]{:S(2)}, u32[]{:S(2)}) collective-permute-start(bf16[196,768]{1,0:T(8,128)(2,1)} %get-tuple-element.68), channel_id=1, source_target_pairs={{0,69},{1,70},{2,71},{3,72},{4,73},{5,74},{6,75},{7,76},{8,77},{9,... | collective-permute-start | bytes 903176 | tf_op jit(solution)/shard_map/ppermute | solution.py:283
  351.3 184.0 %collective-permute-start.23 = (bf16[384,3840]{1,0:T(8,128)(2,1)}, bf16[384,3840]{1,0:T(8,128)(2,1)}, u32[]{:S(2)}, u32[]{:S(2)}) collective-permute-start(bf16[384,3840]{1,0:T(8,128)(2,1)} %fusion.16), channel_id=1, source_target_pairs={{0,64},{64,0},{1,65},{65,1},{2,66},{66,2},{3,67},{67,3},{4,68},{68... | collective-permute-start | bytes 8847368 | tf_op jit(solution)/shard_map/ppermute | solution.py:89
  359.3 23.0 %collective-permute-start.17 = (bf16[2,4,24,2432]{3,2,1,0:T(8,128)(2,1)S(1)}, bf16[2,4,24,2432]{3,2,1,0:T(8,128)(2,1)S(1)}, u32[]{:S(2)}, u32[]{:S(2)}) collective-permute-start(bf16[2,4,24,2432]{3,2,1,0:T(8,128)(2,1)S(1)} %constant_dynamic-slice_fusion.17), channel_id=1, source_target_pairs={{0,48},{48,0},{16,32},{32,16},{1,49},{49,1},{17,33},{33,17},{2,50}... | collective-permute-start | bytes 2801672 | tf_op jit(solution)/shard_map/ppermute | solution.py:79
  382.3 23.3 %collective-permute-start.4 = (bf16[196,768]{1,0:T(8,128)(2,1)S(1)}, bf16[196,768]{1,0:T(8,128)(2,1)S(1)}, u32[]{:S(2)}, u32[]{:S(2)}) collective-permute-start(bf16[196,768]{1,0:T(8,128)(2,1)S(1)} %copy-done.47), channel_id=1, source_target_pairs={{0,68},{1,69},{2,70},{3,71},{4,72},{5,73},{6,74},{7,75},{8,76},{9,... | collective-permute-start | bytes 903176 | tf_op jit(solution)/shard_map/ppermute | solution.py:283
  385.3 40.2 %collective-permute-start.3 = (bf16[196,768]{1,0:T(8,128)(2,1)S(1)}, bf16[196,768]{1,0:T(8,128)(2,1)S(1)}, u32[]{:S(2)}, u32[]{:S(2)}) collective-permute-start(bf16[196,768]{1,0:T(8,128)(2,1)S(1)} %copy-done.46), channel_id=1, source_target_pairs={{0,67},{1,68},{2,69},{3,70},{4,71},{5,72},{6,73},{7,74},{8,75},{9,... | collective-permute-start | bytes 903176 | tf_op jit(solution)/shard_map/ppermute | solution.py:283
  390.6 143.5 %collective-permute-start.18 = (bf16[1,4,24,2432]{3,2,1,0:T(8,128)(2,1)}, bf16[1,4,24,2432]{3,2,1,0:T(8,128)(2,1)}, u32[]{:S(2)}, u32[]{:S(2)}) collective-permute-start(bf16[1,4,24,2432]{3,2,1,0:T(8,128)(2,1)} %constant_dynamic-slice_fusion.16), channel_id=1, source_target_pairs={{0,16},{16,0},{32,48},{48,32},{1,17},{17,1},{33,49},{49,33},{2,18}... | collective-permute-start | bytes 1400840 | tf_op jit(solution)/shard_map/ppermute | solution.py:79
  391.8 42.0 %collective-permute-start.2 = (bf16[196,768]{1,0:T(8,128)(2,1)S(1)}, bf16[196,768]{1,0:T(8,128)(2,1)S(1)}, u32[]{:S(2)}, u32[]{:S(2)}) collective-permute-start(bf16[196,768]{1,0:T(8,128)(2,1)S(1)} %copy-done.45), channel_id=1, source_target_pairs={{0,66},{1,67},{2,68},{3,69},{4,70},{5,71},{6,72},{7,73},{8,74},{9,... | collective-permute-start | bytes 903176 | tf_op jit(solution)/shard_map/ppermute | solution.py:283
  405.6 29.9 %collective-permute-start.1 = (bf16[196,768]{1,0:T(8,128)(2,1)S(1)}, bf16[196,768]{1,0:T(8,128)(2,1)S(1)}, u32[]{:S(2)}, u32[]{:S(2)}) collective-permute-start(bf16[196,768]{1,0:T(8,128)(2,1)S(1)} %copy-done.44), channel_id=1, source_target_pairs={{0,65},{1,66},{2,67},{3,68},{4,69},{5,70},{6,71},{7,72},{8,73},{9,... | collective-permute-start | bytes 903176 | tf_op jit(solution)/shard_map/ppermute | solution.py:283
  433.8 116.0 %collective-permute-start.30 = (bf16[384,4096]{0,1:T(8,128)(2,1)}, bf16[384,4096]{0,1:T(8,128)(2,1)}, u32[]{:S(2)}, u32[]{:S(2)}) collective-permute-start(bf16[384,4096]{0,1:T(8,128)(2,1)} %constant_dynamic-slice_fusion.5), channel_id=1, source_target_pairs={{0,64},{64,0},{1,65},{65,1},{2,66},{66,2},{3,67},{67,3},{4,68},{68... | collective-permute-start | bytes 9437192 | tf_op jit(solution)/shard_map/ppermute | solution.py:89
  546.0 35.4 %collective-permute-start.24 = (bf16[4,2,24,3840]{3,2,1,0:T(8,128)(2,1)}, bf16[4,2,24,3840]{3,2,1,0:T(8,128)(2,1)}, u32[]{:S(2)}, u32[]{:S(2)}) collective-permute-start(bf16[4,2,24,3840]{3,2,1,0:T(8,128)(2,1)} %constant_dynamic-slice_fusion.11), channel_id=1, source_target_pairs={{0,12},{12,0},{4,8},{8,4},{1,13},{13,1},{5,9},{9,5},{2,14},{14,2},... | collective-permute-start | bytes 4423688 | tf_op jit(solution)/shard_map/ppermute | solution.py:79
  559.8 35.2 %collective-permute-start.31 = (bf16[2,4,24,4096]{3,2,1,0:T(8,128)(2,1)}, bf16[2,4,24,4096]{3,2,1,0:T(8,128)(2,1)}, u32[]{:S(2)}, u32[]{:S(2)}) collective-permute-start(bf16[2,4,24,4096]{3,2,1,0:T(8,128)(2,1)} %constant_dynamic-slice_fusion.4), channel_id=1, source_target_pairs={{0,48},{48,0},{16,32},{32,16},{1,49},{49,1},{17,33},{33,17},{2,50}... | collective-permute-start | bytes 4718600 | tf_op jit(solution)/shard_map/ppermute | solution.py:79
  583.7 21.9 %collective-permute-start.25 = (bf16[4,1,24,3840]{3,2,1,0:T(8,128)(2,1)S(1)}, bf16[4,1,24,3840]{3,2,1,0:T(8,128)(2,1)S(1)}, u32[]{:S(2)}, u32[]{:S(2)}) collective-permute-start(bf16[4,1,24,3840]{3,2,1,0:T(8,128)(2,1)S(1)} %constant_dynamic-slice_fusion.10), channel_id=1, source_target_pairs={{0,4},{4,0},{8,12},{12,8},{1,5},{5,1},{9,13},{13,9},{2,6},{6,2},{1... | collective-permute-start | bytes 2211848 | tf_op jit(solution)/shard_map/ppermute | solution.py:79
  597.0 24.3 %collective-permute-start.32 = (bf16[1,4,24,4096]{3,2,1,0:T(8,128)(2,1)S(1)}, bf16[1,4,24,4096]{3,2,1,0:T(8,128)(2,1)S(1)}, u32[]{:S(2)}, u32[]{:S(2)}) collective-permute-start(bf16[1,4,24,4096]{3,2,1,0:T(8,128)(2,1)S(1)} %constant_dynamic-slice_fusion.3), channel_id=1, source_target_pairs={{0,16},{16,0},{32,48},{48,32},{1,17},{17,1},{33,49},{49,33},{2,18}... | collective-permute-start | bytes 2359304 | tf_op jit(solution)/shard_map/ppermute | solution.py:79
  (103 other events, 1138.5 us)
Sparse Core Ops, SparseCore 0:
  38.9 96.6 all-gather.2
